TPU v7x, 32 devices: a whole 2x2x4 slice. The times are simulated.
32 devices in a mesh: band: 2 (over x), tm: 8 (over z, y), space: 2 (over core).
Axes of the slice: x: 2, y: 2, z: 4, core: 2. Of those that a mesh axis runs over, the one named last changes fastest.
Arguments:
- frames: bfloat16 [512, 256, 1024], P('tm', ('band', 'space')), parts along dimension 1, may hold values from -6 to 6
- signal_power: float32 [257], replicated, may hold values from 0.05 to 20
Outputs:
- flow_u: float32 [512, 256, 1024], P('tm', ('band', 'space')), parts along dimension 1
- flow_v: float32 [512, 256, 1024], P('tm', ('band', 'space')), parts along dimension 1
There are 2 independent parts, one for each index of `band`. A program takes and returns all parts, laid end to end along the dimension named above; an argument that names none is the same for every part. Nothing has to cross between parts.
All inputs are finite; a program needn't handle non-finite values.
Results may differ from a plain program's by a relative error of at most 0.0072.
Values may be sent and summed in bfloat16 or wider, within the bound.
A program may use at most 256 MiB of HBM per device.

v0:
```python
import math

import jax
import jax.numpy as jnp
from jax import lax
from jax.sharding import PartitionSpec as P

F = 512
ITERS = 3


def from_behind(block, axis, distance):
    devices = range(lax.axis_size(axis))
    route = [((i - distance) % len(devices), i) for i in devices]
    return lax.ppermute(block, axis, route)


def padded_2(block, sides, width):
    for axis, dim in sides:
        count = lax.axis_size(axis)
        forward = [(i, i + 1) for i in range(count - 1)]
        backward = [(target, source) for source, target in forward]
        low = lax.ppermute(
            lax.slice_in_dim(block, block.shape[dim] - width, None, axis=dim), axis, forward
        )
        high = lax.ppermute(lax.slice_in_dim(block, 0, width, axis=dim), axis, backward)
        block = jnp.concatenate([low, block, high], axis=dim)
    return block


def make_tables():
    freq = jnp.arange(F, dtype=jnp.int32)
    phase = freq[:, None] * freq[None, :] % F
    angle = phase.astype(jnp.float32) * (2.0 * math.pi / F)
    return (jnp.cos(angle).astype(jnp.bfloat16), jnp.sin(angle).astype(jnp.bfloat16))


def full_power(signal_power):
    return jnp.concatenate([signal_power, signal_power[1 : F // 2][::-1]], axis=0)


def wiener_block(block, cosines, sines, power_full):
    real_part = jnp.dot(cosines, block, preferred_element_type=jnp.float32)
    imag_part = jnp.dot(sines, block, preferred_element_type=jnp.float32)
    energy = real_part * real_part + imag_part * imag_part
    noise = jnp.mean(energy[F // 4 : 3 * F // 4], axis=0) / F + 1e-06
    weight = power_full[:, None] / (power_full[:, None] + noise[None, :])
    scaled_real = (weight * real_part).astype(jnp.bfloat16)
    scaled_imag = (weight * imag_part).astype(jnp.bfloat16)
    restored = jnp.dot(cosines, scaled_real, preferred_element_type=jnp.float32)
    restored = restored + jnp.dot(sines, scaled_imag, preferred_element_type=jnp.float32)
    return (restored / F).astype(jnp.bfloat16)


def across_columns(field):
    padded = jnp.pad(field, ((0, 0), (0, 0), (1, 1)))
    return padded[:, :, 2:] - padded[:, :, :-2]


def vertical_mean(extended):
    center = extended[:, 1:-1, :]
    col_pad = jnp.pad(center, ((0, 0), (0, 0), (1, 1)))
    return 0.25 * (
        extended[:, :-2, :] + extended[:, 2:, :] + col_pad[:, :, :-2] + col_pad[:, :, 2:]
    )


def derivatives(extended_pair):
    first = extended_pair[0].astype(jnp.float32)
    second = extended_pair[1].astype(jnp.float32)
    first_mid = first[:, 1:-1, :]
    second_mid = second[:, 1:-1, :]
    grad_x = 0.25 * (across_columns(first_mid) + across_columns(second_mid))
    grad_y = 0.25 * (first[:, 2:, :] - first[:, :-2, :] + (second[:, 2:, :] - second[:, :-2, :]))
    grad_t = second_mid - first_mid
    denom = 1.0 + grad_x * grad_x + grad_y * grad_y
    return (grad_x, grad_y, grad_t, denom)


def shards(frames, signal_power):
    cosines, sines = make_tables()
    power_full = full_power(signal_power)
    gathered = lax.all_to_all(frames, "tm", split_axis=1, concat_axis=0, tiled=True)
    shape_now = gathered.shape
    flat = gathered.reshape(shape_now[0], shape_now[1] * shape_now[2])
    restored = lax.all_to_all(
        wiener_block(flat, cosines, sines, power_full).reshape(shape_now),
        "tm",
        split_axis=0,
        concat_axis=1,
        tiled=True,
    )
    following = from_behind(restored[0], "tm", -1)
    upcoming = jnp.concatenate([restored[1:], following[None]], axis=0)
    frame_pair = jnp.stack([restored, upcoming], axis=0)
    extended_pair = padded_2(frame_pair, (("space", 2),), 1)
    grad_x, grad_y, grad_t, denom = derivatives(extended_pair)
    flow_u = jnp.zeros_like(grad_x)
    flow_v = jnp.zeros_like(grad_x)
    for iteration in range(ITERS):
        if iteration == 0:
            mean_u = vertical_mean(jnp.pad(flow_u, ((0, 0), (1, 1), (0, 0))))
            mean_v = vertical_mean(jnp.pad(flow_v, ((0, 0), (1, 1), (0, 0))))
        else:
            extended_flow = padded_2(jnp.stack([flow_u, flow_v], axis=0), (("space", 2),), 1)
            mean_u = vertical_mean(extended_flow[0])
            mean_v = vertical_mean(extended_flow[1])
        common = (grad_x * mean_u + grad_y * mean_v + grad_t) / denom
        flow_u = mean_u - grad_x * common
        flow_v = mean_v - grad_y * common
    return (flow_u, flow_v)


def solution(mesh):
    in_specs = (P("tm", ("band", "space"), None), P())
    out_specs = (P("tm", ("band", "space"), None), P("tm", ("band", "space"), None))
    return jax.shard_map(shards, mesh=mesh, in_specs=in_specs, out_specs=out_specs, check_vma=False)
```

profile of v0, /device:TPU:13, one launch (start us, length us, event | category | flops | bytes accessed | tf_op | source)
XLA Modules:
  0.0 1096.1 jit_solution(4897787238683026084)
XLA Ops:
  18.3 180.0 %all-to-all-done = bf16[64,64,1024]{2,0,1:T(8,128)(2,1)} async-done(((bf16[64,64,1024]{2,0,1:T(8,128)(2,1)}), bf16[64,64,1024]{2,0,1:T(8,128)(2,1)}, u32[]{:S(2)}, u32[]{:S(2)}) %all-to-all-start) | async-done | bytes 8388640 | tf_op jit(solution)/shard_map/all_to_all | solution.py:83
  198.3 12.1 %copy.8 = bf16[64,8,8,1024]{3,2,0,1:T(8,128)(2,1)} copy(bf16[64,8,8,1024]{3,0,2,1:T(8,128)(2,1)} %bitcast) | data formatting | bytes 16777216 | tf_op jit(solution)/shard_map/all_to_all | solution.py:83
  210.4 17.0 %copy.10 = bf16[64,8,8,1024]{3,1,2,0:T(8,128)(2,1)} copy(bf16[64,8,8,1024]{3,2,1,0:T(8,128)(2,1)} %bitcast.58) | data formatting | bytes 16777216
  227.4 11.7 %fusion.32 = f32[512,8192]{1,0:T(8,128)S(1)} fusion(bf16[512,8192]{1,0:T(8,128)(2,1)} %bitcast.50), kind=kOutput, calls=%fused_computation.92 | convolution fusion | flops 4298899456 | bytes 25165824 | tf_op jit(solution)/shard_map/dot_general | solution.py:44
  239.1 12.0 %fusion.31 = f32[512,8192]{1,0:T(8,128)} fusion(bf16[512,8192]{1,0:T(8,128)(2,1)S(1)} %bitcast.51), kind=kOutput, calls=%fused_computation.91 | convolution fusion | flops 4298899456 | bytes 25165824 | tf_op jit(solution)/shard_map/dot_general | solution.py:43
  255.3 20.4 %fusion.24 = f32[512,8192]{1,0:T(8,128)} fusion(f32[512,8192]{1,0:T(8,128)} %fusion.31, f32[8192]{0:T(1024)S(1)} %multiply_add_fusion.3, f32[512]{0:T(512)S(1)} %pad_maximum_fusion.9), kind=kOutput, calls=%fused_computation.70 | convolution fusion | flops 4315676672 | bytes 33589248 | tf_op jit(solution)/shard_map/dot_general | solution.py:50
  275.7 22.5 %multiply_convert_fusion = bf16[512,8192]{1,0:T(8,128)(2,1)} fusion(f32[512,8192]{1,0:T(8,128)} %fusion.24, f32[512,8192]{1,0:T(8,128)} %copy-done.7, f32[8192]{0:T(1024)S(1)} %multiply_add_fusion.3, f32[512]{0:T(512)S(1)} %pad_maximum_fusion.9), kind=kOutput, calls=%fused_computation.55 | convolution fusion | flops 4328259584 | bytes 41977856 | tf_op jit(solution)/shard_map/dot_general | solution.py:51
  298.2 16.5 %copy.11 = bf16[64,8,8,1024]{3,2,1,0:T(8,128)(2,1)} copy(bf16[64,8,8,1024]{3,1,2,0:T(8,128)(2,1)} %bitcast.61) | data formatting | bytes 16777216
  314.7 187.1 %all_to_all.30 = bf16[512,8,1024]{2,1,0:T(8,128)(2,1)} all-to-all(bf16[512,8,1024]{2,1,0:T(8,128)(2,1)} %bitcast.59), channel_id=1, replica_groups=mesh['band'=2,'tm'=8,'space'=2] {'tm'}, dimensions={0} | all-to-all | bytes 16777216 | tf_op jit(solution)/shard_map/all_to_all | solution.py:86
  539.9 24.9 %pad_maximum_fusion.2 = bf16[2,64,66,1024]{3,2,1,0:T(8,128)(2,1)} fusion(bf16[2,64,1,1024]{3,2,1,0:T(2,128)(2,1)S(1)} %collective-permute-done.2, bf16[1,64,64,1024]{3,2,1,0:T(8,128)(2,1)S(1)} %copy-done.8, bf16[1,64,64,1024]{3,2,1,0:T(8,128)(2,1)S(1)} %bitcast.57, bf16[2,64,1,1024]{3,2,1,0:T(2,128)(2,1)S(1)} %collective-permute-done.1), kind=kLoop, calls=%fused_computation.6 | loop fusion | flops 69206016 | bytes 34603008 | tf_op jit(solution)/shard_map/concatenate | solution.py:27
  564.8 15.9 %fusion.19 = (f32[64,66,1024]{2,1,0:T(8,128)S(1)}, f32[64,66,1024]{2,1,0:T(8,128)}) fusion(bf16[2,64,66,1024]{3,2,1,0:T(8,128)(2,1)} %pad_maximum_fusion.2), kind=kLoop, calls=%fused_computation.61 | loop fusion | flops 8650752 | bytes 51904512 | tf_op jit(solution)/shard_map/convert_element_type | solution.py:70
  592.4 13.0 %slice.224 = f32[64,64,1024]{2,1,0:T(8,128)} slice(f32[64,66,1024]{2,1,0:T(8,128)} %get-tuple-element.21), slice={[0:64], [1:65], [0:1024]} | slice | bytes 33554432 | tf_op jit(solution)/shard_map/slice | solution.py:71
  605.4 87.5 %subtract_bitcast_fusion.3 = (f32[1,64,64,1024]{3,2,1,0:T(8,128)}, f32[64,64,1024]{2,1,0:T(8,128)}, f32[64,64,1024]{2,1,0:T(8,128)}, f32[64,64,1024]{2,1,0:T(8,128)}) fusion(f32[1024]{0:T(1024)S(1)} %get-tuple-element.27, f32[1024]{0:T(1024)S(1)} %get-tuple-element.26, f32[64]{0:T(128)S(1)} %fusion.33, f32[64,66,1024]{2,1,0:T(8,128)} %get-tuple-element.21, ...), kind=kLoop, calls=%fused_computation.52 | loop fusion | flops 92274688 | bytes 201335040 | tf_op jit(solution)/shard_map/stack | solution.py:105
  692.9 23.8 %subtract_bitcast_fusion.2 = f32[1,64,64,1024]{3,2,1,0:T(8,128)} fusion(f32[64,64,1024]{2,1,0:T(8,128)} %get-tuple-element.11, f32[1024]{0:T(1024)S(1)} %get-tuple-element.27, f32[1024]{0:T(1024)S(1)} %get-tuple-element.26, f32[64]{0:T(128)S(1)} %fusion.33, f32[64,64,1024]{2,1,0:T(8,128)} %get-tuple-element.10, f32[64,64,1024]{2,1,0:T(8,128)} %get-tuple-element.9), kind=kLoop, calls=%fused_computation.51 | loop fusion | flops 54525952 | bytes 67117312 | tf_op jit(solution)/shard_map/stack | solution.py:105
  728.3 20.3 %pad_maximum_fusion = f32[2,64,66,1024]{3,2,1,0:T(8,128)} fusion(f32[2,64,1,1024]{3,2,1,0:T(1,128)S(1)} %collective-permute-done.4, f32[1,64,64,1024]{3,2,1,0:T(8,128)} %subtract_bitcast_fusion.2, f32[1,64,64,1024]{3,2,1,0:T(8,128)S(1)} %copy-done.4, f32[2,64,1,1024]{3,2,1,0:T(1,128)S(1)} %collective-permute-done.3), kind=kLoop, calls=%fused_computation | loop fusion | flops 25952256 | bytes 69206016 | tf_op jit(solution)/shard_map/concatenate | solution.py:27
  748.6 20.6 %slice_bitcast_fusion.2 = (f32[64,66,1024]{2,1,0:T(8,128)S(1)}, f32[64,66,1024]{2,1,0:T(8,128)}) fusion(f32[2,64,66,1024]{3,2,1,0:T(8,128)} %pad_maximum_fusion), kind=kLoop, calls=%fused_computation.4 | loop fusion | bytes 69206016 | tf_op jit(solution)/shard_map/squeeze | solution.py:107
  780.7 13.0 %slice.234 = f32[64,64,1024]{2,1,0:T(8,128)} slice(f32[64,66,1024]{2,1,0:T(8,128)} %get-tuple-element.15), slice={[0:64], [1:65], [0:1024]} | slice | bytes 33554432 | tf_op jit(solution)/shard_map/slice | solution.py:61
  793.7 79.9 %subtract_bitcast_fusion.1 = (f32[1,64,64,1024]{3,2,1,0:T(8,128)}, f32[64,64,1024]{2,1,0:T(8,128)}, f32[64,64,1024]{2,1,0:T(8,128)}) fusion(f32[64,64,1024]{2,1,0:T(8,128)} %get-tuple-element.10, f32[64,64,1024]{2,1,0:T(8,128)} %get-tuple-element.11, f32[64,64,1024]{2,1,0:T(8,128)} %get-tuple-element.9, f32[64,64,1024]{2,1,0:T(8,128)} %slice.234, ...), kind=kLoop, calls=%fused_computation.49 | loop fusion | flops 79691776 | bytes 201326592 | tf_op jit(solution)/shard_map/stack | solution.py:105
  873.7 34.7 %subtract_bitcast_fusion = f32[1,64,64,1024]{3,2,1,0:T(8,128)} fusion(f32[64,64,1024]{2,1,0:T(8,128)} %get-tuple-element.7, f32[64,64,1024]{2,1,0:T(8,128)} %get-tuple-element.11, f32[64,64,1024]{2,1,0:T(8,128)} %get-tuple-element.10, f32[64,64,1024]{2,1,0:T(8,128)} %get-tuple-element.9, f32[64,64,1024]{2,1,0:T(8,128)} %get-tuple-element.6), kind=kLoop, calls=%fused_computation.48 | loop fusion | flops 46137344 | bytes 100663296 | tf_op jit(solution)/shard_map/stack | solution.py:105
  921.8 14.0 %pad_maximum_fusion.1 = f32[2,64,66,1024]{3,2,1,0:T(8,128)} fusion(f32[2,64,1,1024]{3,2,1,0:T(1,128)S(1)} %collective-permute-done.6, f32[1,64,64,1024]{3,2,1,0:T(8,128)S(1)} %copy-done.6, f32[1,64,64,1024]{3,2,1,0:T(8,128)S(1)} %copy-done.5, f32[2,64,1,1024]{3,2,1,0:T(1,128)S(1)} %collective-permute-done.5), kind=kLoop, calls=%fused_computation.1 | loop fusion | flops 25952256 | bytes 69206016 | tf_op jit(solution)/shard_map/concatenate | solution.py:27
  935.8 20.6 %slice_bitcast_fusion.1 = (f32[64,66,1024]{2,1,0:T(8,128)S(1)}, f32[64,66,1024]{2,1,0:T(8,128)}) fusion(f32[2,64,66,1024]{3,2,1,0:T(8,128)} %pad_maximum_fusion.1), kind=kLoop, calls=%fused_computation.3 | loop fusion | bytes 69206016 | tf_op jit(solution)/shard_map/squeeze | solution.py:106
  968.1 13.0 %slice.246 = f32[64,64,1024]{2,1,0:T(8,128)} slice(f32[64,66,1024]{2,1,0:T(8,128)} %get-tuple-element.13), slice={[0:64], [1:65], [0:1024]} | slice | bytes 33554432 | tf_op jit(solution)/shard_map/slice | solution.py:61
  981.1 79.9 %multiply_subtract_fusion = (f32[64,64,1024]{2,1,0:T(8,128)}, f32[64,64,1024]{2,1,0:T(8,128)}, f32[64,64,1024]{2,1,0:T(8,128)}) fusion(f32[64,64,1024]{2,1,0:T(8,128)} %get-tuple-element.11, f32[64,64,1024]{2,1,0:T(8,128)} %get-tuple-element.10, f32[64,64,1024]{2,1,0:T(8,128)} %get-tuple-element.9, f32[64,64,1024]{2,1,0:T(8,128)} %slice.246, ...), kind=kLoop, calls=%fused_computation.45 | loop fusion | flops 79691776 | bytes 201326592 | tf_op jit(solution)/shard_map/sub | solution.py:110
  1060.9 34.7 %multiply_subtract_fusion.1 = f32[64,64,1024]{2,1,0:T(8,128)} fusion(f32[64,64,1024]{2,1,0:T(8,128)} %get-tuple-element.4, f32[64,64,1024]{2,1,0:T(8,128)} %get-tuple-element.10, f32[64,64,1024]{2,1,0:T(8,128)} %get-tuple-element.11, f32[64,64,1024]{2,1,0:T(8,128)} %get-tuple-element.9, f32[64,64,1024]{2,1,0:T(8,128)} %get-tuple-element.3), kind=kLoop, calls=%fused_computation.46 | loop fusion | flops 46137344 | bytes 100663296 | tf_op jit(solution)/shard_map/sub | solution.py:109
  (61 shorter events, 119.5 us)
Async XLA Ops:
  0.6 17.4 %copy-start.9 = (f32[257]{0:T(512)S(1)}, f32[257]{0:T(512)}, u32[]{:S(2)}) copy-start(f32[257]{0:T(512)} %param.3) | copy-start | bytes 3088
  12.1 186.2 %all-to-all-start = ((bf16[64,64,1024]{2,0,1:T(8,128)(2,1)}), bf16[64,64,1024]{2,0,1:T(8,128)(2,1)}, u32[]{:S(2)}, u32[]{:S(2)}) async-start(bf16[64,64,1024]{2,0,1:T(8,128)(2,1)} %copy.7), calls=%async_computation | async-start | bytes 16777216 | tf_op jit(solution)/shard_map/all_to_all | solution.py:83
  227.4 11.7 %copy-start.3 = (bf16[64,8,8,1024]{3,1,2,0:T(8,128)(2,1)S(1)}, bf16[64,8,8,1024]{3,1,2,0:T(8,128)(2,1)}, u32[]{:S(2)}) copy-start(bf16[64,8,8,1024]{3,1,2,0:T(8,128)(2,1)} %copy.10) | copy-start | bytes 25165828
  239.1 12.0 %copy-start.7 = (f32[512,8192]{1,0:T(8,128)}, f32[512,8192]{1,0:T(8,128)S(1)}, u32[]{:S(2)}) copy-start(f32[512,8192]{1,0:T(8,128)S(1)} %fusion.32) | copy-start | bytes 50331652
  511.0 10.2 collective-permute-start
  521.2 18.7 %slice-start = ((s8[8388608]{0:T(1024)(128)(4,1)}), s8[4194304]{0:T(1024)(128)(4,1)S(1)}, s32[]{:S(2)}) async-start(s8[8388608]{0:T(1024)(128)(4,1)} %bitcast.55), calls=%async_computation.2 | async-start | bytes 8388608
  528.8 11.1 %copy-start.8 = (bf16[1,64,64,1024]{3,2,1,0:T(8,128)(2,1)S(1)}, bf16[1,64,64,1024]{3,2,1,0:T(8,128)(2,1)}, u32[]{:S(2)}) copy-start(bf16[1,64,64,1024]{3,2,1,0:T(8,128)(2,1)} %maximum_bitcast_fusion) | copy-start | bytes 25165828
  528.8 11.1 %slice-start.1 = ((s8[8388608]{0:T(1024)(128)(4,1)}), s8[4194304]{0:T(1024)(128)(4,1)S(1)}, s32[]{:S(2)}) async-start(s8[8388608]{0:T(1024)(128)(4,1)} %bitcast.55), calls=%async_computation.3 | async-start | bytes 8388608
  532.2 6.4 collective-permute-start.1
  533.8 6.1 collective-permute-start.2
  580.7 11.7 %copy-start = (f32[64,66,1024]{2,1,0:T(8,128)}, f32[64,66,1024]{2,1,0:T(8,128)S(1)}, u32[]{:S(2)}) copy-start(f32[64,66,1024]{2,1,0:T(8,128)S(1)} %get-tuple-element.20) | copy-start | bytes 51904516
  692.9 26.3 %copy-start.4 = (f32[1,64,64,1024]{3,2,1,0:T(8,128)S(1)}, f32[1,64,64,1024]{3,2,1,0:T(8,128)}, u32[]{:S(2)}) copy-start(f32[1,64,64,1024]{3,2,1,0:T(8,128)} %get-tuple-element.8) | copy-start | bytes 50331652
  722.4 4.6 collective-permute-start.3
  723.7 4.6 collective-permute-start.4
  769.3 11.4 %copy-start.1 = (f32[64,66,1024]{2,1,0:T(8,128)}, f32[64,66,1024]{2,1,0:T(8,128)S(1)}, u32[]{:S(2)}) copy-start(f32[64,66,1024]{2,1,0:T(8,128)S(1)} %get-tuple-element.14) | copy-start | bytes 51904516
  908.4 12.6 %copy-start.5 = (f32[1,64,64,1024]{3,2,1,0:T(8,128)S(1)}, f32[1,64,64,1024]{3,2,1,0:T(8,128)}, u32[]{:S(2)}) copy-start(f32[1,64,64,1024]{3,2,1,0:T(8,128)} %get-tuple-element.5) | copy-start | bytes 50331652
  908.4 13.4 %copy-start.6 = (f32[1,64,64,1024]{3,2,1,0:T(8,128)S(1)}, f32[1,64,64,1024]{3,2,1,0:T(8,128)}, u32[]{:S(2)}) copy-start(f32[1,64,64,1024]{3,2,1,0:T(8,128)} %subtract_bitcast_fusion) | copy-start | bytes 50331652
  914.1 5.4 collective-permute-start.5
  915.6 5.3 collective-permute-start.6
  956.4 11.6 %copy-start.2 = (f32[64,66,1024]{2,1,0:T(8,128)}, f32[64,66,1024]{2,1,0:T(8,128)S(1)}, u32[]{:S(2)}) copy-start(f32[64,66,1024]{2,1,0:T(8,128)S(1)} %get-tuple-element.12) | copy-start | bytes 51904516
where the time goes:
time: 1100 us
  other arithmetic  440 us (40%)
  local copies, waits for them, and re-layouts  193 us (18%)
  blocking collectives  187 us (17%)
  waiting for transfers between devices  184 us (17%)
  matrix products  66.6 us (6%)
  starting transfers between devices  24 us (2%)
    another operation x4, other arithmetic, shards(): jnp.stack([flow_u, flow_v], axis=0)  226 us
    all_to_all x1, blocking collectives, shards(): lax.all_to_all(wiener_block(flat, cosines, sines, power_full).reshape(sha...  187 us
    all_to_all x1, waiting for transfers between devices, shards(): lax.all_to_all(frames, 'tm', split_axis=1, concat_axis=0, tiled=True)  180 us
    sub x1, other arithmetic, shards(): flow_v = mean_v - grad_y * common  79.9 us
    unnamed x29, local copies, waits for them, and re-layouts  61.2 us
    concatenate x3, other arithmetic, padded_2(): block = jnp.concatenate([low, block, high], axis=dim)  59.2 us
    slice x5, local copies, waits for them, and re-layouts, vertical_mean(): center = extended[:, 1:-1, :]  40.7 us
    sub x1, other arithmetic, shards(): flow_u = mean_u - grad_x * common  34.7 us
  transfers between devices with their start and end apart: 8, of which 4 were waited for; matrix products, arithmetic and copies ran while one was open for 1% of the time, Pallas kernels for 0%

commit v1 on v0

--- a/solution.py
+++ b/solution.py
@@ -1,8 +1,12 @@
+import functools
 import math
 
 import jax
 import jax.numpy as jnp
+import numpy as np
 from jax import lax
+from jax.experimental import pallas as pl
+from jax.experimental.pallas import tpu as pltpu
 from jax.sharding import PartitionSpec as P
 
 F = 512
@@ -77,7 +81,7 @@
     return (grad_x, grad_y, grad_t, denom)
 
 
-def shards(frames, signal_power):
+def plain_shards(frames, signal_power):
     cosines, sines = make_tables()
     power_full = full_power(signal_power)
     gathered = lax.all_to_all(frames, "tm", split_axis=1, concat_axis=0, tiled=True)
@@ -111,6 +115,271 @@
     return (flow_u, flow_v)
 
 
+MESH = pl.DeviceIdType.MESH
+
+
+def real_basis():
+    freq = np.arange(F)
+    angle = (freq[:, None] * freq[None, :] % F).astype(np.float32) * np.float32(2.0 * math.pi / F)
+    half = F // 2
+    basis = np.concatenate(
+        [np.cos(angle[:half]), np.cos(angle[half : half + 1]), np.sin(angle[1:half])], axis=0
+    ).astype(jnp.bfloat16)
+    weight = np.full((F,), 2.0 / F, np.float32)
+    weight[0] = weight[half] = 1.0 / F
+    inverse = (basis.astype(np.float32) * weight[:, None]).T.astype(jnp.bfloat16)
+    return basis, np.ascontiguousarray(inverse)
+
+
+def filter_tile(block, basis, inverse, power):
+    half, quarter = F // 2, F // 4
+    spectrum = jnp.dot(basis, block, preferred_element_type=jnp.float32)
+    energy = spectrum * spectrum
+    upper = energy[quarter:half] + energy[half + quarter :]
+    total = 2.0 * jnp.sum(upper, axis=0, keepdims=True) - upper[0:1] + energy[half : half + 1]
+    noise = total * (1.0 / (half * F)) + 1e-06
+    scaled = (power / (power + noise) * spectrum).astype(jnp.bfloat16)
+    return jnp.dot(inverse, scaled, preferred_element_type=jnp.float32).astype(jnp.bfloat16)
+
+
+def exchange_kernel(n, x_ref, basis_ref, inverse_ref, power_ref, out_ref, gath, filt, s1, r1, s2, r2):
+    me = lax.axis_index("tm")
+    rows, frames, columns = x_ref.shape
+    chunks = rows // n
+    tile = power_ref.shape[1]
+
+    barrier = pltpu.get_barrier_semaphore()
+    for d in range(1, n):
+        peer = lax.rem(me + d, n)
+        pl.semaphore_signal(barrier, inc=1, device_id={"tm": peer}, device_id_type=MESH)
+    pl.semaphore_wait(barrier, n - 1)
+
+    def span(device):
+        return pl.ds(pl.multiple_of(device * frames, frames), frames)
+
+    def scatter(c, carry):
+        pltpu.make_async_copy(x_ref.at[c * n + me], gath.at[c, span(me)], r1.at[c]).start()
+        for d in range(1, n):
+            peer = lax.rem(me + d, n)
+            pltpu.make_async_remote_copy(
+                src_ref=x_ref.at[c * n + peer],
+                dst_ref=gath.at[c, span(me)],
+                send_sem=s1.at[c],
+                recv_sem=r1.at[c],
+                device_id={"tm": peer},
+                device_id_type=MESH,
+            ).start()
+        return carry
+
+    lax.fori_loop(0, chunks, scatter, 0)
+
+    def work(c, carry):
+        pltpu.make_async_copy(gath.at[c], gath.at[c], r1.at[c]).wait()
+
+        def one(i, carry):
+            cols = pl.ds(pl.multiple_of(i * tile, tile), tile)
+            filt[c, :, cols] = filter_tile(
+                gath[c, :, cols], basis_ref[...], inverse_ref[...], power_ref[...]
+            )
+            return carry
+
+        lax.fori_loop(0, columns // tile, one, 0)
+        pltpu.make_async_copy(filt.at[c, span(me)], out_ref.at[c * n + me], r2.at[c]).start()
+        for d in range(1, n):
+            peer = lax.rem(me + d, n)
+            pltpu.make_async_remote_copy(
+                src_ref=filt.at[c, span(peer)],
+                dst_ref=out_ref.at[c * n + me],
+                send_sem=s2.at[c],
+                recv_sem=r2.at[c],
+                device_id={"tm": peer},
+                device_id_type=MESH,
+            ).start()
+        return carry
+
+    lax.fori_loop(0, chunks, work, 0)
+
+    def drain(c, carry):
+        sent = gath.at[c, pl.ds(0, (n - 1) * frames)]
+        pltpu.make_async_copy(sent, sent, s1.at[c]).wait()
+        pltpu.make_async_copy(sent, sent, s2.at[c]).wait()
+        landed = out_ref.at[pl.ds(c * n, n)]
+        pltpu.make_async_copy(landed, landed, r2.at[c]).wait()
+        return carry
+
+    lax.fori_loop(0, chunks, drain, 0)
+
+
+def exchange_and_filter(by_rows, signal_power):
+    n = lax.axis_size("tm")
+    rows, frames, columns = by_rows.shape
+    chunks, half, tile = rows // n, F // 2, 256
+    basis, inverse = real_basis()
+    power = jnp.concatenate([signal_power, signal_power[1:half]], axis=0)
+    power = jnp.broadcast_to(power[:, None], (F, tile))
+    vmem = pl.BlockSpec(memory_space=pltpu.VMEM)
+    hbm = pl.BlockSpec(memory_space=pl.ANY)
+    return pl.pallas_call(
+        functools.partial(exchange_kernel, n),
+        out_shape=jax.ShapeDtypeStruct(by_rows.shape, jnp.bfloat16),
+        in_specs=[hbm, vmem, vmem, vmem],
+        out_specs=hbm,
+        scratch_shapes=[
+            pltpu.VMEM((chunks, F, columns), jnp.bfloat16),
+            pltpu.VMEM((chunks, F, columns), jnp.bfloat16),
+        ]
+        + [pltpu.SemaphoreType.DMA((chunks,))] * 4,
+        compiler_params=pltpu.CompilerParams(
+            collective_id=0, has_side_effects=True, vmem_limit_bytes=40 * 2**20
+        ),
+        cost_estimate=pl.CostEstimate(
+            flops=4 * F * rows * frames * columns,
+            bytes_accessed=4 * rows * frames * columns,
+            transcendentals=0,
+        ),
+        name="exchange",
+    )(by_rows, jnp.asarray(basis), jnp.asarray(inverse), power)
+
+
+STRIP = 16
+LAG = 8
+
+
+def flow_kernel(flag_ref, body_ref, low_ref, high_ref, next_ref, u_ref, v_ref, *ring):
+    total, shift, gx_r, gy_r, gt_r, inv_r, u1_r, v1_r, u2_r, v2_r, u3_r, v3_r = ring
+    rows, strip, columns = body_ref.shape
+    groups = rows // LAG + 1
+    lane = lax.broadcasted_iota(jnp.int32, (strip, columns), 1)
+    frame = lax.broadcasted_iota(jnp.int32, (strip, columns), 0)
+    at_low, at_high, at_last = lane == 0, lane == columns - 1, frame == strip - 1
+    low_flag, high_flag = flag_ref[0], flag_ref[1]
+
+    def left(x):
+        return jnp.where(at_low, 0.0, pltpu.roll(x, 1, 1))
+
+    def right(x):
+        return jnp.where(at_high, 0.0, pltpu.roll(x, columns - 1, 1))
+
+    def mean(ref, i):
+        center = ref[i % LAG]
+        return 0.25 * (ref[(i - 1) % LAG] + ref[(i + 1) % LAG] + left(center) + right(center))
+
+    def step(u_prev, v_prev, i):
+        mean_u, mean_v = mean(u_prev, i), mean(v_prev, i)
+        j = i % LAG
+        gx, gy = gx_r[j], gy_r[j]
+        common = (gx * mean_u + gy * mean_v + gt_r[j]) * inv_r[j]
+        return mean_u - gx * common, mean_v - gy * common
+
+    def group(g, carry):
+        for i in range(LAG):
+            at = jnp.clip(g * LAG + i - 5, 0, rows - 1)
+            first = body_ref[at]
+            if 2 <= i <= 4:
+                first = jnp.where(g == 0, low_ref[i - 2], first)
+            if i >= 5:
+                first = jnp.where(g == groups - 1, high_ref[i - 5], first)
+            first = first.astype(jnp.float32)
+            extended = jnp.clip(g * LAG + i - 2, 0, rows + 5)
+            after = next_ref[0, pl.ds(extended, 1), :]
+            second = jnp.where(at_last, after, pltpu.roll(first, strip - 1, 0))
+            total[(i - 2) % LAG] = first + second
+            shift[(i - 2) % LAG] = second - first
+            k = (i - 3) % LAG
+            center = total[k]
+            gx = 0.25 * (right(center) - left(center))
+            gy = 0.25 * (total[(i - 2) % LAG] - total[(i - 4) % LAG])
+            gt = shift[k]
+            inv = 1.0 / (1.0 + gx * gx + gy * gy)
+            common = gt * inv
+            gx_r[k], gy_r[k], gt_r[k], inv_r[k] = gx, gy, gt, inv
+            u1_r[k] = -gx * common
+            v1_r[k] = -gy * common
+            k = (i - 4) % LAG
+            u2, v2 = step(u1_r, v1_r, i - 4)
+            if i == 6:
+                keep = jnp.where(g == 0, low_flag, 1.0)
+                u2, v2 = u2 * keep, v2 * keep
+            if i == 7:
+                keep = jnp.where(g == groups - 1, high_flag, 1.0)
+                u2, v2 = u2 * keep, v2 * keep
+            u2_r[k], v2_r[k] = u2, v2
+            u3_r[i], v3_r[i] = step(u2_r, v2_r, i - 5)
+
+        @pl.when(g > 0)
+        def _():
+            place = pl.ds(pl.multiple_of((g - 1) * LAG, LAG), LAG)
+            for b in range(0, strip, 8):
+                u_ref[b : b + 8, place, :] = jnp.swapaxes(u3_r[:, b : b + 8, :], 0, 1)
+                v_ref[b : b + 8, place, :] = jnp.swapaxes(v3_r[:, b : b + 8, :], 0, 1)
+
+        return carry
+
+    lax.fori_loop(0, groups, group, 0)
+
+
+def flow(body, low, high, following, flags):
+    rows, frames, columns = body.shape
+    out = jax.ShapeDtypeStruct((frames, rows, columns), jnp.float32)
+    out_spec = pl.BlockSpec((STRIP, rows, columns), lambda i: (i, 0, 0))
+
+    def strip_of(height):
+        return pl.BlockSpec((height, STRIP, columns), lambda i: (0, i, 0))
+
+    return pl.pallas_call(
+        flow_kernel,
+        grid=(frames // STRIP,),
+        out_shape=(out, out),
+        in_specs=[
+            pl.BlockSpec(memory_space=pltpu.SMEM),
+            strip_of(rows),
+            strip_of(3),
+            strip_of(3),
+            pl.BlockSpec((1, following.shape[1], columns), lambda i: (i, 0, 0)),
+        ],
+        out_specs=(out_spec, out_spec),
+        scratch_shapes=[pltpu.VMEM((LAG, STRIP, columns), jnp.float32)] * 12,
+        compiler_params=pltpu.CompilerParams(vmem_limit_bytes=56 * 2**20),
+        cost_estimate=pl.CostEstimate(
+            flops=100 * rows * frames * columns,
+            bytes_accessed=10 * rows * frames * columns,
+            transcendentals=0,
+        ),
+        name="flow",
+    )(flags, body, low, high, following)
+
+
+def neighbours(block, dim, width):
+    count = lax.axis_size("space")
+    forward = [(i, i + 1) for i in range(count - 1)]
+    backward = [(target, source) for source, target in forward]
+    size = block.shape[dim]
+    low = lax.ppermute(
+        lax.slice_in_dim(block, size - width, size, axis=dim), "space", forward
+    )
+    high = lax.ppermute(lax.slice_in_dim(block, 0, width, axis=dim), "space", backward)
+    return low, high
+
+
+def shards(frames, signal_power):
+    n = lax.axis_size("tm")
+    count, rows, columns = frames.shape
+    fits = n > 1 and count % STRIP == 0 and rows % n == 0 and rows % LAG == 0
+    if not (fits and columns % 256 == 0):
+        return plain_shards(frames, signal_power)
+    by_rows = jnp.transpose(frames, (1, 0, 2))
+    body = exchange_and_filter(by_rows, signal_power)
+    following = from_behind(body[:, 0], "tm", -1)
+    firsts = [body[:, b] for b in range(STRIP, count, STRIP)] + [following]
+    firsts = jnp.stack(firsts, axis=0)
+    low, high = neighbours(body, 0, 3)
+    low_first, high_first = neighbours(firsts, 1, 3)
+    firsts = jnp.concatenate([low_first, firsts, high_first], axis=1).astype(jnp.float32)
+    here, last = lax.axis_index("space"), lax.axis_size("space") - 1
+    flags = jnp.stack([here > 0, here < last]).astype(jnp.float32)
+    return flow(body, low, high, firsts, flags)
+
+
 def solution(mesh):
     in_specs = (P("tm", ("band", "space"), None), P())
     out_specs = (P("tm", ("band", "space"), None), P("tm", ("band", "space"), None))

time: 1100 us -> 467 us (0.42)
  other arithmetic: 440 us -> 2.67 us
  Pallas kernels: 0 us -> 432 us
  blocking collectives: 187 us -> 0 us
  waiting for transfers between devices: 184 us -> 4.8 us
  local copies, waits for them, and re-layouts: 193 us -> 15.2 us
  matrix products: 66.6 us -> 0 us
  starting transfers between devices: 24 us -> 9.3 us
    pallas_call x0 -> x2, Pallas kernels: none -> 432 us  [the longest x1 365 us: exchange_and_filter(): pl.pallas_call(functools.partial(exchange_kernel, n), out_shape=jax.Shape...]
    another operation x5 -> x0, other arithmetic: 234 us -> none  [the longest x4 226 us: shards(): jnp.stack([flow_u, flow_v], axis=0)]
    all_to_all x1 -> x0, blocking collectives: 187 us -> none  [shards(): lax.all_to_all(wiener_block(flat, cosines, sines, power_full).reshape(sha...]
    all_to_all x1 -> x0, waiting for transfers between devices: 180 us -> none  [shards(): lax.all_to_all(frames, 'tm', split_axis=1, concat_axis=0, tiled=True)]
    sub x2 -> x0, other arithmetic: 115 us -> none  [the longest x1 79.9 us: shards(): flow_v = mean_v - grad_y * common]
    slice x10 -> x3, local copies, waits for them, and re-layouts: 69.5 us -> 1.78 us  [the longest x1 0.97 us: shards(): firsts = [body[:, b] for b in range(STRIP, count, STRIP)] + [following]]
    dot_general x4 -> x0, matrix products: 66.6 us -> none  [the longest x1 22.5 us: wiener_block(): jnp.dot(sines, scaled_imag, preferred_element_type=jnp.float32)]
    concatenate x4 -> x1, other arithmetic: 59.3 us -> 0.76 us  [exchange_and_filter(): power = jnp.concatenate([signal_power, signal_power[1:half]], axis=0)]
  transfers between devices with their start and end apart: 8 -> 5, of which waited for: 4 -> 2; matrix products, arithmetic and copies ran while one was open for 1% -> 1% of each run, Pallas kernels for 0% -> 0%
where the time goes in v1:
time: 467 us; the launch traced here: 465 us
  Pallas kernels  432 us (93%)
  local copies, waits for them, and re-layouts  15.2 us (3%)
  starting transfers between devices  9.3 us (2%)
  waiting for transfers between devices  4.8 us (1%)
    pallas_call x1, Pallas kernels, exchange_and_filter(): pl.pallas_call(functools.partial(exchange_kernel, n), out_shape=jax.Shape...  365 us
    pallas_call x1, Pallas kernels, flow(): pl.pallas_call(flow_kernel, grid=(frames // STRIP,), out_shape=(out, out)...  66.6 us
    unnamed x13, local copies, waits for them, and re-layouts  13.2 us
  transfers between devices with their start and end apart: 5, of which 2 were waited for; matrix products, arithmetic and copies ran while one was open for 1% of the time, Pallas kernels for 0%

profile of v1, /device:TPU:13, one launch (start us, length us, event | category | flops | bytes accessed | tf_op | source)
XLA Modules:
  0.0 464.6 jit_solution(3380748103648408384)
XLA Ops:
  0.6 0.8 slice.27
  1.4 0.8 pad_maximum_fusion.4
  2.1 11.6 %copy.20 = bf16[64,64,1024]{2,0,1:T(8,128)(2,1)} copy(bf16[64,64,1024]{2,1,0:T(8,128)(2,1)} %param.4) | data formatting | bytes 16777216 | tf_op args[0]
  13.7 0.1 broadcast_in_dim.2.power_ref
  13.9 0.0 copy-done.1
  13.9 365.3 %exchange.1.body_ref = bf16[64,64,1024]{2,1,0:T(8,128)(2,1)S(1)} custom-call(bf16[64,64,1024]{2,1,0:T(8,128)(2,1)} %bitcast.16, bf16[512,512]{1,0:T(8,128)(2,1)S(1)} %copy-done.2, bf16[512,512]{1,0:T(8,128)(2,1)S(1)} %copy-done.1, f32[512,256]{1,0:T(8,128)S(1)} %broadcast_in_dim.2.power_ref), custom_call_target="tpu_custom_call" | custom-call | flops 8589934592 | bytes 16777216 | tf_op jit(solution)/shard_map/exchange/pallas_call | solution.py:222
  379.1 0.1 fusion.1
  379.2 2.4 collective-permute-start.1
  381.7 1.3 collective-permute-start
  383.0 1.0 fusion
  384.0 0.1 collective-permute-start.2
  384.1 0.1 copy_bitcast_fusion.2
  384.2 4.6 collective-permute-done.2
  388.8 1.3 collective-permute-start.3
  390.1 4.2 collective-permute-start.4
  394.3 0.6 add_convert_fusion.flag_ref
  394.9 0.0 collective-permute-done.3
  394.9 0.2 collective-permute-done.4
  395.2 1.3 maximum_convert_fusion.next_ref
  396.5 0.0 collective-permute-done.1.high_ref
  396.5 0.0 collective-permute-done.low_ref
  396.5 0.7 copy-done.3
  397.2 0.8 copy-done.4
  398.0 66.6 %flow.1 = (f32[64,64,1024]{2,1,0:T(8,128)}, f32[64,64,1024]{2,1,0:T(8,128)}) custom-call(f32[2]{0:T(128)} %add_convert_fusion.flag_ref, bf16[64,64,1024]{2,1,0:T(8,128)(2,1)} %copy-done, bf16[3,64,1024]{2,1,0:T(8,128)(2,1)} %copy-done.4, bf16[3,64,1024]{2,1,0:T(8,128)(2,1)} %copy-done.3, f32[4,70,1024]{2,1,0:T(8,128)} %maximum_convert_fusion.next_ref), custom_call_target="tpu_custom_call" | custom-call | flops 419430400 | bytes 41943040 | tf_op jit(solution)/shard_map/flow/pallas_call | solution.py:329
  (10 shorter events, 0.1 us)
Async XLA Ops:
  2.1 11.7 %copy-start.1 = (bf16[512,512]{1,0:T(8,128)(2,1)S(1)}, bf16[512,512]{1,0:T(8,128)(2,1)}, u32[]{:S(2)}) copy-start(bf16[512,512]{1,0:T(8,128)(2,1)} %constant.13.clone.inverse_ref) | copy-start | bytes 1572868
  2.1 11.7 %copy-start.2 = (bf16[512,512]{1,0:T(8,128)(2,1)S(1)}, bf16[512,512]{1,0:T(8,128)(2,1)}, u32[]{:S(2)}) copy-start(bf16[512,512]{1,0:T(8,128)(2,1)} %constant.12.clone.basis_ref) | copy-start | bytes 1572868
  379.1 3.8 copy-start
  379.2 17.3 %collective-permute-start.1 = (bf16[3,64,1024]{2,1,0:T(8,128)(2,1)S(1)}, bf16[3,64,1024]{2,1,0:T(8,128)(2,1)S(1)}, u32[]{:S(2)}, u32[]{:S(2)}) collective-permute-start(bf16[3,64,1024]{2,1,0:T(8,128)(2,1)S(1)} %get-tuple-element.6), channel_id=1, source_target_pairs={{1,0},{3,2},{5,4},{7,6},{9,8},{11,10},{13,12},{15,14},{17,16},{19,... | collective-permute-start | bytes 1179656 | tf_op jit(solution)/shard_map/ppermute | solution.py:360
  381.7 14.8 %collective-permute-start = (bf16[3,64,1024]{2,1,0:T(8,128)(2,1)S(1)}, bf16[3,64,1024]{2,1,0:T(8,128)(2,1)S(1)}, u32[]{:S(2)}, u32[]{:S(2)}) collective-permute-start(bf16[3,64,1024]{2,1,0:T(8,128)(2,1)S(1)} %get-tuple-element.7), channel_id=1, source_target_pairs={{0,1},{2,3},{4,5},{6,7},{8,9},{10,11},{12,13},{14,15},{16,17},{18,... | collective-permute-start | bytes 1179656 | tf_op jit(solution)/shard_map/ppermute | solution.py:357
  384.0 4.8 %collective-permute-start.2 = (bf16[64,1024]{1,0:T(8,128)(2,1)S(1)}, bf16[64,1024]{1,0:T(8,128)(2,1)S(1)}, u32[]{:S(2)}, u32[]{:S(2)}) collective-permute-start(bf16[64,1024]{1,0:T(8,128)(2,1)S(1)} %bitcast.21), channel_id=1, source_target_pairs={{2,0},{4,2},{6,4},{8,6},{10,8},{12,10},{14,12},{0,14},{3,1},{5,3},... | collective-permute-start | bytes 393224 | tf_op jit(solution)/shard_map/ppermute | solution.py:19
  388.8 6.1 %collective-permute-start.3 = (bf16[4,3,1024]{2,1,0:T(4,128)(2,1)S(1)}, bf16[4,3,1024]{2,1,0:T(4,128)(2,1)S(1)}, u32[]{:S(2)}, u32[]{:S(2)}) collective-permute-start(bf16[4,3,1024]{2,1,0:T(4,128)(2,1)S(1)} %get-tuple-element.8), channel_id=1, source_target_pairs={{0,1},{2,3},{4,5},{6,7},{8,9},{10,11},{12,13},{14,15},{16,17},{18,... | collective-permute-start | bytes 73736 | tf_op jit(solution)/shard_map/ppermute | solution.py:357
  390.1 5.1 %collective-permute-start.4 = (bf16[4,3,1024]{2,1,0:T(4,128)(2,1)S(1)}, bf16[4,3,1024]{2,1,0:T(4,128)(2,1)S(1)}, u32[]{:S(2)}, u32[]{:S(2)}) collective-permute-start(bf16[4,3,1024]{2,1,0:T(4,128)(2,1)S(1)} %get-tuple-element.9), channel_id=1, source_target_pairs={{1,0},{3,2},{5,4},{7,6},{9,8},{11,10},{13,12},{15,14},{17,16},{19,... | collective-permute-start | bytes 73736 | tf_op jit(solution)/shard_map/ppermute | solution.py:360
  396.5 0.7 copy-start.3
  397.2 0.8 copy-start.4

commit v2 on v0

--- a/solution.py
+++ b/solution.py
@@ -1,8 +1,12 @@
+import functools
 import math
 
 import jax
 import jax.numpy as jnp
+import numpy as np
 from jax import lax
+from jax.experimental import pallas as pl
+from jax.experimental.pallas import tpu as pltpu
 from jax.sharding import PartitionSpec as P
 
 F = 512
@@ -77,7 +81,7 @@
     return (grad_x, grad_y, grad_t, denom)
 
 
-def shards(frames, signal_power):
+def plain_shards(frames, signal_power):
     cosines, sines = make_tables()
     power_full = full_power(signal_power)
     gathered = lax.all_to_all(frames, "tm", split_axis=1, concat_axis=0, tiled=True)
@@ -111,6 +115,366 @@
     return (flow_u, flow_v)
 
 
+MESH = pl.DeviceIdType.MESH
+
+
+def real_basis():
+    freq = np.arange(F)
+    angle = (freq[:, None] * freq[None, :] % F).astype(np.float32) * np.float32(2.0 * math.pi / F)
+    half = F // 2
+    basis = np.concatenate(
+        [np.cos(angle[:half]), np.cos(angle[half : half + 1]), np.sin(angle[1:half])], axis=0
+    ).astype(jnp.bfloat16)
+    weight = np.full((F,), 2.0 / F, np.float32)
+    weight[0] = weight[half] = 1.0 / F
+    inverse = (basis.astype(np.float32) * weight[:, None]).T.astype(jnp.bfloat16)
+    return basis, np.ascontiguousarray(inverse)
+
+
+STRIP = 16
+RING = 4
+TILE = 256
+
+
+def filter_tile(block, basis, inverse, power):
+    half, quarter = F // 2, F // 4
+    spectrum = jnp.dot(basis, block, preferred_element_type=jnp.float32)
+    energy = spectrum * spectrum
+    upper = energy[quarter:half] + energy[half + quarter :]
+    total = 2.0 * jnp.sum(upper, axis=0, keepdims=True) - upper[0:1] + energy[half : half + 1]
+    noise = total * (1.0 / (half * F)) + 1e-06
+    scaled = (power / (power + noise) * spectrum).astype(jnp.bfloat16)
+    return jnp.dot(inverse, scaled, preferred_element_type=jnp.float32)
+
+
+def fused_kernel(n, x_ref, basis_ref, inverse_ref, power_ref, u_ref, v_ref, *scratch):
+    (xin, xt, gath, filt, land, edge, after, land_h, after_h) = scratch[:9]
+    (total, shift, gx_r, gy_r, gt_r, inv_r, u1_r, v1_r, u2_r, v2_r) = scratch[9:19]
+    (sx, s1, r1, s2, r2, s3, r3, sh, rh, so) = scratch[19:]
+    me, side = lax.axis_index("tm"), lax.axis_index("space")
+    frames, rows, columns = x_ref.shape
+    chunks, blocks, strips = rows // n, rows // STRIP, frames // STRIP
+    per_block = chunks // blocks
+
+    def physical(row):
+        return side * row + (1 - side) * (rows - 1 - row)
+
+    def block_rows(m):
+        first = side * m + (1 - side) * (blocks - 1 - m)
+        return pl.ds(pl.multiple_of(first * STRIP, STRIP), STRIP)
+
+    def span(device):
+        return pl.ds(pl.multiple_of(device * frames, frames), frames)
+
+    def fetch(m):
+        slot = lax.rem(m, 2)
+        return pltpu.make_async_copy(x_ref.at[:, block_rows(m), :], xin.at[slot], sx.at[slot])
+
+    fetch(0).start()
+    fetch(1).start()
+    barrier = pltpu.get_barrier_semaphore()
+    for d in range(1, n):
+        peer = lax.rem(me + d, n)
+        pl.semaphore_signal(barrier, inc=1, device_id={"tm": peer}, device_id_type=MESH)
+    pl.semaphore_signal(barrier, inc=1, device_id={"space": 1 - side}, device_id_type=MESH)
+    pl.semaphore_wait(barrier, n)
+
+    def to_peer(src, dst, send, recv, peer):
+        return pltpu.make_async_remote_copy(
+            src_ref=src,
+            dst_ref=dst,
+            send_sem=send,
+            recv_sem=recv,
+            device_id={"tm": peer},
+            device_id_type=MESH,
+        )
+
+    def scatter(m, carry):
+        fetch(m).wait()
+        slot = lax.rem(m, 2)
+        per_row = columns // TILE
+
+        def turn(i, carry):
+            cols = pl.ds(pl.multiple_of(lax.rem(i, per_row) * TILE, TILE), TILE)
+            part = pl.ds(pl.multiple_of(i // per_row * STRIP, STRIP), STRIP)
+            piece = xin[slot, part, :, cols].astype(jnp.float32)
+            xt[block_rows(m), part, cols] = jnp.swapaxes(piece, 0, 1).astype(jnp.bfloat16)
+            return carry
+
+        lax.fori_loop(0, strips * per_row, turn, 0)
+
+        @pl.when(m + 2 < blocks)
+        def _():
+            fetch(m + 2).start()
+
+        for k in range(per_block):
+            c = m * per_block + k
+            own = xt.at[physical(c * n + me)]
+            pltpu.make_async_copy(own, gath.at[c, span(me)], r1.at[c]).start()
+            for d in range(1, n):
+                peer = lax.rem(me + d, n)
+                src = xt.at[physical(c * n + peer)]
+                to_peer(src, gath.at[c, span(me)], s1.at[c], r1.at[c], peer).start()
+        return carry
+
+    lax.fori_loop(0, blocks, scatter, 0)
+
+    def work(c, carry):
+        pltpu.make_async_copy(gath.at[c], gath.at[c], r1.at[c]).wait()
+
+        def one(i, carry):
+            cols = pl.ds(pl.multiple_of(i * TILE, TILE), TILE)
+            restored = filter_tile(
+                gath[c, :, cols], basis_ref[...], inverse_ref[...], power_ref[...]
+            ).astype(jnp.bfloat16)
+            filt[c, :, cols] = restored
+            for p in range(n):
+                at = p * frames
+                edge[c, p, :, cols] = restored[at : at + STRIP].astype(jnp.float32)[0:1]
+            return carry
+
+        lax.fori_loop(0, columns // TILE, one, 0)
+        row = c * n + me
+        pltpu.make_async_copy(filt.at[c, span(me)], land.at[row], r2.at[c]).start()
+        own_edge = edge.at[c, lax.rem(me + 1, n)]
+        pltpu.make_async_copy(own_edge, after.at[row], r3.at[c]).start()
+        for d in range(1, n):
+            peer = lax.rem(me + d, n)
+            to_peer(filt.at[c, span(peer)], land.at[row], s2.at[c], r2.at[c], peer).start()
+            src = edge.at[c, lax.rem(peer + 1, n)]
+            to_peer(src, after.at[row], s3.at[c], r3.at[c], peer).start()
+        return carry
+
+    lax.fori_loop(0, chunks, work, 0)
+
+    lane = lax.broadcasted_iota(jnp.int32, (STRIP, columns), 1)
+    frame = lax.broadcasted_iota(jnp.int32, (STRIP, columns), 0)
+    at_low, at_high, at_last = lane == 0, lane == columns - 1, frame == STRIP - 1
+    quarter = (2 * side - 1).astype(jnp.float32) * 0.25
+
+    def left(x):
+        return jnp.where(at_low, 0.0, pltpu.roll(x, 1, 1))
+
+    def right(x):
+        return jnp.where(at_high, 0.0, pltpu.roll(x, columns - 1, 1))
+
+    def iterate(b, u_prev, v_prev, low, here, high):
+        def mean(ref):
+            center = ref[b, here]
+            return 0.25 * (ref[b, low] + ref[b, high] + left(center) + right(center))
+
+        mean_u, mean_v = mean(u_prev), mean(v_prev)
+        gx, gy = gx_r[b, here], gy_r[b, here]
+        common = (gx * mean_u + gy * mean_v + gt_r[b, here]) * inv_r[b, here]
+        return mean_u - gx * common, mean_v - gy * common
+
+    def step(b, e, first, second, outside=False):
+        k0, k1, k2, k3 = (lax.rem(e + RING - back, RING) for back in range(4))
+        total[b, k0] = first + second
+        shift[b, k0] = second - first
+        center = total[b, k1]
+        gx = 0.25 * (right(center) - left(center))
+        gy = quarter * (total[b, k0] - total[b, k2])
+        gt = shift[b, k1]
+        inv = 1.0 / (1.0 + gx * gx + gy * gy)
+        common = gt * inv
+        gx_r[b, k1], gy_r[b, k1], gt_r[b, k1], inv_r[b, k1] = gx, gy, gt, inv
+        u1_r[b, k1] = -gx * common
+        v1_r[b, k1] = -gy * common
+        u2, v2 = iterate(b, u1_r, v1_r, k3, k2, k1)
+        if outside:
+            u2, v2 = jnp.zeros_like(u2), jnp.zeros_like(v2)
+        u2_r[b, k2], v2_r[b, k2] = u2, v2
+        u3, v3 = iterate(b, u2_r, v2_r, k0, k3, k2)
+        q = jnp.maximum(e - 6, 0)
+        start = lax.rem(q, n) * frames + b * STRIP
+        place = pl.ds(pl.multiple_of(start, STRIP), STRIP)
+        gath[q // n, place, :] = u3.astype(jnp.bfloat16)
+        filt[q // n, place, :] = v3.astype(jnp.bfloat16)
+
+    def pair(b, ref, after_ref, row):
+        first = ref[row, pl.ds(pl.multiple_of(b * STRIP, STRIP), STRIP), :].astype(jnp.float32)
+        later = jnp.minimum(b + 1, strips - 1)
+        later = pl.ds(pl.multiple_of(later * STRIP, STRIP), STRIP)
+        inside = ref[row, later, :].astype(jnp.float32)[0:1]
+        upcoming = jnp.where(b == strips - 1, after_ref[row], inside)
+        second = jnp.where(at_last, upcoming, pltpu.roll(first, STRIP - 1, 0))
+        return first, second
+
+    def emit(q):
+        def send(src, dst, sem):
+            block = src.at[q // n, span(lax.rem(q, n))]
+            pltpu.make_async_copy(block, dst.at[physical(q)], sem).start()
+
+        send(gath, u_ref, so.at[0])
+        send(filt, v_ref, so.at[1])
+
+    def arrive(c):
+        pltpu.make_async_copy(filt.at[c], filt.at[c], r2.at[c]).wait()
+        landed = after.at[pl.ds(c * n, n)]
+        pltpu.make_async_copy(landed, landed, r3.at[c]).wait()
+        sent = filt.at[c, pl.ds(0, (n - 1) * frames)]
+        pltpu.make_async_copy(sent, sent, s2.at[c]).wait()
+
+    def to_side(src, dst, k):
+        return pltpu.make_async_remote_copy(
+            src_ref=src,
+            dst_ref=dst,
+            send_sem=sh.at[k],
+            recv_sem=rh.at[k],
+            device_id={"space": 1 - side},
+            device_id_type=MESH,
+        )
+
+    arrive(0)
+    halo = (
+        to_side(land.at[pl.ds(0, 3)], land_h, 0),
+        to_side(after.at[pl.ds(0, 3)], after_h, 1),
+    )
+    for copy in halo:
+        copy.start()
+    for copy in halo:
+        copy.wait()
+
+    def group(g, carry):
+        @pl.when(g > 0)
+        def _():
+            arrive(g)
+
+        def strip(b, carry):
+            @pl.when(g == 0)
+            def _():
+                def before(e, carry):
+                    step(b, e, *pair(b, land_h, after_h, 2 - e))
+                    return carry
+
+                lax.fori_loop(0, 3, before, 0)
+
+            def inner(i, carry):
+                row = g * n + i
+                step(b, row + 3, *pair(b, land, after, row))
+                return carry
+
+            lax.fori_loop(0, n, inner, 0)
+            return carry
+
+        lax.fori_loop(0, strips, strip, 0)
+
+        def out(i, carry):
+            q = g * n - 3 + i
+
+            @pl.when(q >= 0)
+            def _():
+                emit(q)
+
+            return carry
+
+        lax.fori_loop(0, n, out, 0)
+        return carry
+
+    lax.fori_loop(0, chunks, group, 0)
+
+    def finish(b, carry):
+        zero = jnp.zeros((STRIP, columns), jnp.float32)
+        for i in range(3):
+            step(b, rows + 3 + i, zero, zero, outside=i == 2)
+        return carry
+
+    lax.fori_loop(0, strips, finish, 0)
+    for i in range(3):
+        emit(rows - 3 + i)
+
+    def drain(c, carry):
+        sent = filt.at[c, pl.ds(0, (n - 1) * frames)]
+        pltpu.make_async_copy(sent, sent, s1.at[c]).wait()
+        sent = after.at[pl.ds(0, n - 1)]
+        pltpu.make_async_copy(sent, sent, s3.at[c]).wait()
+        return carry
+
+    lax.fori_loop(0, chunks, drain, 0)
+    pltpu.make_async_copy(u_ref, u_ref, so.at[0]).wait()
+    pltpu.make_async_copy(v_ref, v_ref, so.at[1]).wait()
+
+
+def exchange_and_flow(frames, signal_power):
+    n = lax.axis_size("tm")
+    count, rows, columns = frames.shape
+    chunks, half, strips = rows // n, F // 2, count // STRIP
+    basis, inverse = real_basis()
+    power = jnp.concatenate([signal_power, signal_power[1:half]], axis=0)
+    power = jnp.broadcast_to(power[:, None], (F, TILE))
+    vmem = pl.BlockSpec(memory_space=pltpu.VMEM)
+    hbm = pl.BlockSpec(memory_space=pl.ANY)
+    out = jax.ShapeDtypeStruct((rows, count, columns), jnp.bfloat16)
+    dma = pltpu.SemaphoreType.DMA
+    return pl.pallas_call(
+        functools.partial(fused_kernel, n),
+        out_shape=(out, out),
+        in_specs=[hbm, vmem, vmem, vmem],
+        out_specs=(hbm, hbm),
+        scratch_shapes=[
+            pltpu.VMEM((2, count, STRIP, columns), jnp.bfloat16),
+            pltpu.VMEM((rows, count, columns), jnp.bfloat16),
+            pltpu.VMEM((chunks, F, columns), jnp.bfloat16),
+            pltpu.VMEM((chunks, F, columns), jnp.bfloat16),
+            pltpu.VMEM((rows, count, columns), jnp.bfloat16),
+            pltpu.VMEM((chunks, n, 1, columns), jnp.float32),
+            pltpu.VMEM((rows, 1, columns), jnp.float32),
+            pltpu.VMEM((3, count, columns), jnp.bfloat16),
+            pltpu.VMEM((3, 1, columns), jnp.float32),
+        ]
+        + [pltpu.VMEM((strips, RING, STRIP, columns), jnp.float32)] * 10
+        + [dma((2,))]
+        + [dma((chunks,))] * 6
+        + [dma((2,))] * 3,
+        compiler_params=pltpu.CompilerParams(
+            collective_id=0, has_side_effects=True, vmem_limit_bytes=60 * 2**20
+        ),
+        cost_estimate=pl.CostEstimate(
+            flops=4 * F * rows * count * columns,
+            bytes_accessed=6 * rows * count * columns,
+            transcendentals=0,
+        ),
+        name="exchange",
+    )(frames, jnp.asarray(basis), jnp.asarray(inverse), power)
+
+
+def widen_kernel(u_in, v_in, u_out, v_out):
+    for b in range(0, u_in.shape[2], TILE):
+        cols = slice(b, b + TILE)
+        u_out[:, :, cols] = jnp.swapaxes(u_in[:, :, cols].astype(jnp.float32), 0, 1)
+        v_out[:, :, cols] = jnp.swapaxes(v_in[:, :, cols].astype(jnp.float32), 0, 1)
+
+
+def widen(u, v):
+    rows, count, columns = u.shape
+    out = jax.ShapeDtypeStruct((count, rows, columns), jnp.float32)
+    in_spec = pl.BlockSpec((STRIP, STRIP, columns), lambda i, j: (j, i, 0))
+    out_spec = pl.BlockSpec((STRIP, STRIP, columns), lambda i, j: (i, j, 0))
+    return pl.pallas_call(
+        widen_kernel,
+        grid=(count // STRIP, rows // STRIP),
+        out_shape=(out, out),
+        in_specs=[in_spec, in_spec],
+        out_specs=(out_spec, out_spec),
+        compiler_params=pltpu.CompilerParams(vmem_limit_bytes=40 * 2**20),
+        cost_estimate=pl.CostEstimate(
+            flops=0, bytes_accessed=12 * rows * count * columns, transcendentals=0
+        ),
+        name="widen",
+    )(u, v)
+
+
+def shards(frames, signal_power):
+    n = lax.axis_size("tm")
+    count, rows, columns = frames.shape
+    fits = n >= 3 and count % STRIP == 0 and rows % (2 * STRIP) == 0 and rows % n == 0
+    fits = fits and STRIP % n == 0 and columns % TILE == 0 and lax.axis_size("space") == 2
+    if not fits:
+        return plain_shards(frames, signal_power)
+    return widen(*exchange_and_flow(frames, signal_power))
+
+
 def solution(mesh):
     in_specs = (P("tm", ("band", "space"), None), P())
     out_specs = (P("tm", ("band", "space"), None), P("tm", ("band", "space"), None))

time: 1100 us -> 447 us (0.41)
  Pallas kernels: 0 us -> 440 us
  other arithmetic: 440 us -> 0.76 us
  local copies, waits for them, and re-layouts: 193 us -> 5.06 us
  blocking collectives: 187 us -> 0 us
  waiting for transfers between devices: 184 us -> 0 us
  matrix products: 66.6 us -> 0 us
  starting transfers between devices: 24 us -> 0 us
    pallas_call x0 -> x2, Pallas kernels: none -> 440 us  [the longest x1 422 us: exchange_and_flow(): pl.pallas_call(functools.partial(fused_kernel, n), out_shape=(out, out),...]
    another operation x5 -> x0, other arithmetic: 234 us -> none  [the longest x4 226 us: shards(): jnp.stack([flow_u, flow_v], axis=0)]
    all_to_all x1 -> x0, blocking collectives: 187 us -> none  [shards(): lax.all_to_all(wiener_block(flat, cosines, sines, power_full).reshape(sha...]
    all_to_all x1 -> x0, waiting for transfers between devices: 180 us -> none  [shards(): lax.all_to_all(frames, 'tm', split_axis=1, concat_axis=0, tiled=True)]
    sub x2 -> x0, other arithmetic: 115 us -> none  [the longest x1 79.9 us: shards(): flow_v = mean_v - grad_y * common]
    slice x10 -> x1, local copies, waits for them, and re-layouts: 69.5 us -> 0.76 us  [exchange_and_flow(): power = jnp.concatenate([signal_power, signal_power[1:half]], axis=0)]
    dot_general x4 -> x0, matrix products: 66.6 us -> none  [the longest x1 22.5 us: wiener_block(): jnp.dot(sines, scaled_imag, preferred_element_type=jnp.float32)]
    concatenate x4 -> x1, other arithmetic: 59.3 us -> 0.76 us  [exchange_and_flow(): power = jnp.concatenate([signal_power, signal_power[1:half]], axis=0)]
  transfers between devices with their start and end apart: 8 -> 0, of which waited for: 4 -> 0; matrix products, arithmetic and copies ran while one was open for 1% -> 0% of each run, Pallas kernels for 0% -> 0%
where the time goes in v2:
time: 447 us
  Pallas kernels  440 us (98%)
  local copies, waits for them, and re-layouts  5.06 us (1%)
    pallas_call x1, Pallas kernels, exchange_and_flow(): pl.pallas_call(functools.partial(fused_kernel, n), out_shape=(out, out),...  422 us
    pallas_call x1, Pallas kernels, widen(): pl.pallas_call(widen_kernel, grid=(count // STRIP, rows // STRIP), out_sh...  18.6 us

profile of v2, /device:TPU:13, one launch (start us, length us, event | category | flops | bytes accessed | tf_op | source)
XLA Modules:
  0.0 446.6 jit_solution(882446795367934507)
XLA Ops:
  0.6 0.8 slice.3
  1.4 0.8 pad_maximum_fusion
  2.1 0.9 broadcast_in_dim.2.power_ref
  3.1 421.6 %exchange.1 = (bf16[64,64,1024]{2,1,0:T(8,128)(2,1)}, bf16[64,64,1024]{2,1,0:T(8,128)(2,1)}) custom-call(bf16[64,64,1024]{2,1,0:T(8,128)(2,1)} %x_ref.1, bf16[512,512]{1,0:T(8,128)(2,1)} %constant.4.clone.basis_ref, bf16[512,512]{1,0:T(8,128)(2,1)} %constant.5.clone.inverse_ref, f32[512,256]{1,0:T(8,128)} %broadcast_in_dim.2.power_ref), custom_call_target="tpu_custom_call" | custom-call | flops 8589934592 | bytes 25165824 | tf_op jit(solution)/shard_map/exchange/pallas_call | solution.py:410
  424.7 0.0 copy-start
  424.7 3.4 copy-done
  428.1 18.6 %widen.1 = (f32[64,64,1024]{2,1,0:T(8,128)}, f32[64,64,1024]{2,1,0:T(8,128)}) custom-call(bf16[64,64,1024]{2,1,0:T(8,128)(2,1)S(1)} %copy-done, bf16[64,64,1024]{2,1,0:T(8,128)(2,1)} %get-tuple-element.5.v_in), custom_call_target="tpu_custom_call" | custom-call | bytes 50331648 | tf_op jit(solution)/shard_map/widen/pallas_call | solution.py:454
Async XLA Ops:
  424.7 3.4 copy-start

commit v3 on v2

--- a/solution.py
+++ b/solution.py
@@ -134,6 +134,7 @@
 STRIP = 16
 RING = 4
 TILE = 256
+DELAY = 2
 
 
 def filter_tile(block, basis, inverse, power):
@@ -219,7 +220,7 @@
 
     lax.fori_loop(0, blocks, scatter, 0)
 
-    def work(c, carry):
+    def work(c):
         pltpu.make_async_copy(gath.at[c], gath.at[c], r1.at[c]).wait()
 
         def one(i, carry):
@@ -243,20 +244,23 @@
             to_peer(filt.at[c, span(peer)], land.at[row], s2.at[c], r2.at[c], peer).start()
             src = edge.at[c, lax.rem(peer + 1, n)]
             to_peer(src, after.at[row], s3.at[c], r3.at[c], peer).start()
-        return carry
-
-    lax.fori_loop(0, chunks, work, 0)
-
-    lane = lax.broadcasted_iota(jnp.int32, (STRIP, columns), 1)
+
+    lane = lax.broadcasted_iota(jnp.int32, (STRIP, 128), 1)
     frame = lax.broadcasted_iota(jnp.int32, (STRIP, columns), 0)
-    at_low, at_high, at_last = lane == 0, lane == columns - 1, frame == STRIP - 1
+    at_low, at_high, at_last = lane == 0, lane == 127, frame == STRIP - 1
     quarter = (2 * side - 1).astype(jnp.float32) * 0.25
 
     def left(x):
-        return jnp.where(at_low, 0.0, pltpu.roll(x, 1, 1))
+        turned = pltpu.roll(x, 1, 1)
+        return jnp.concatenate(
+            [jnp.where(at_low, 0.0, turned[:, :128]), turned[:, 128:]], axis=1
+        )
 
     def right(x):
-        return jnp.where(at_high, 0.0, pltpu.roll(x, columns - 1, 1))
+        turned = pltpu.roll(x, columns - 1, 1)
+        return jnp.concatenate(
+            [turned[:, :-128], jnp.where(at_high, 0.0, turned[:, -128:])], axis=1
+        )
 
     def iterate(b, u_prev, v_prev, low, here, high):
         def mean(ref):
@@ -326,20 +330,19 @@
             device_id_type=MESH,
         )
 
-    arrive(0)
-    halo = (
-        to_side(land.at[pl.ds(0, 3)], land_h, 0),
-        to_side(after.at[pl.ds(0, 3)], after_h, 1),
-    )
-    for copy in halo:
-        copy.start()
-    for copy in halo:
-        copy.wait()
-
-    def group(g, carry):
-        @pl.when(g > 0)
+    def group(g):
+        arrive(g)
+
+        @pl.when(g == 0)
         def _():
-            arrive(g)
+            halo = (
+                to_side(land.at[pl.ds(0, 3)], land_h, 0),
+                to_side(after.at[pl.ds(0, 3)], after_h, 1),
+            )
+            for copy in halo:
+                copy.start()
+            for copy in halo:
+                copy.wait()
 
         def strip(b, carry):
             @pl.when(g == 0)
@@ -370,9 +373,19 @@
             return carry
 
         lax.fori_loop(0, n, out, 0)
+
+    def turn_of(c, carry):
+        @pl.when(c < chunks)
+        def _():
+            work(c)
+
+        @pl.when(c >= DELAY)
+        def _():
+            group(c - DELAY)
+
         return carry
 
-    lax.fori_loop(0, chunks, group, 0)
+    lax.fori_loop(0, chunks + DELAY, turn_of, 0)
 
     def finish(b, carry):
         zero = jnp.zeros((STRIP, columns), jnp.float32)
@@ -457,7 +470,7 @@
         out_shape=(out, out),
         in_specs=[in_spec, in_spec],
         out_specs=(out_spec, out_spec),
-        compiler_params=pltpu.CompilerParams(vmem_limit_bytes=40 * 2**20),
+        compiler_params=pltpu.CompilerParams(vmem_limit_bytes=60 * 2**20),
         cost_estimate=pl.CostEstimate(
             flops=0, bytes_accessed=12 * rows * count * columns, transcendentals=0
         ),

time: 447 us -> 429 us (0.960)
  Pallas kernels: 440 us -> 424 us
    pallas_call x1, Pallas kernels: 422 us -> 402 us  [exchange_and_flow(): pl.pallas_call(functools.partial(fused_kernel, n), out_shape=(out, out),...]
where the time goes in v3:
time: 429 us; the launch traced here: 427 us
  Pallas kernels  424 us (99%)
    pallas_call x1, Pallas kernels, exchange_and_flow(): pl.pallas_call(functools.partial(fused_kernel, n), out_shape=(out, out),...  402 us
    pallas_call x1, Pallas kernels, widen(): pl.pallas_call(widen_kernel, grid=(count // STRIP, rows // STRIP), out_sh...  21.7 us

profile of v3, /device:TPU:13, one launch (start us, length us, event | category | flops | bytes accessed | tf_op | source)
XLA Modules:
  0.0 427.2 jit_solution(28806081670533521)
XLA Ops:
  0.6 0.8 slice.3
  1.4 0.8 pad_maximum_fusion
  2.1 0.9 broadcast_in_dim.2.power_ref
  3.1 402.4 %exchange.1 = (bf16[64,64,1024]{2,1,0:T(8,128)(2,1)}, bf16[64,64,1024]{2,1,0:T(8,128)(2,1)}) custom-call(bf16[64,64,1024]{2,1,0:T(8,128)(2,1)} %x_ref.1, bf16[512,512]{1,0:T(8,128)(2,1)} %constant.4.clone.basis_ref, bf16[512,512]{1,0:T(8,128)(2,1)} %constant.5.clone.inverse_ref, f32[512,256]{1,0:T(8,128)} %broadcast_in_dim.2.power_ref), custom_call_target="tpu_custom_call" | custom-call | flops 8589934592 | bytes 25165824 | tf_op jit(solution)/shard_map/exchange/pallas_call | solution.py:423
  405.5 21.7 %widen.1 = (f32[64,64,1024]{2,1,0:T(8,128)}, f32[64,64,1024]{2,1,0:T(8,128)}) custom-call(bf16[64,64,1024]{2,1,0:T(8,128)(2,1)} %get-tuple-element.4.u_in, bf16[64,64,1024]{2,1,0:T(8,128)(2,1)} %get-tuple-element.5.v_in), custom_call_target="tpu_custom_call" | custom-call | bytes 50331648 | tf_op jit(solution)/shard_map/widen/pallas_call | solution.py:467

commit v4 on v3

--- a/solution.py
+++ b/solution.py
@@ -190,7 +190,7 @@
             device_id_type=MESH,
         )
 
-    def scatter(m, carry):
+    def scatter(m):
         fetch(m).wait()
         slot = lax.rem(m, 2)
         per_row = columns // TILE
@@ -216,9 +216,6 @@
                 peer = lax.rem(me + d, n)
                 src = xt.at[physical(c * n + peer)]
                 to_peer(src, gath.at[c, span(me)], s1.at[c], r1.at[c], peer).start()
-        return carry
-
-    lax.fori_loop(0, blocks, scatter, 0)
 
     def work(c):
         pltpu.make_async_copy(gath.at[c], gath.at[c], r1.at[c]).wait()
@@ -374,10 +371,22 @@
 
         lax.fori_loop(0, n, out, 0)
 
+    def begin(m, carry):
+        scatter(m)
+        return carry
+
+    lax.fori_loop(0, 2, begin, 0)
+
     def turn_of(c, carry):
         @pl.when(c < chunks)
         def _():
             work(c)
+
+        m = (c + 1) // per_block + 1
+
+        @pl.when(jnp.logical_and(lax.rem(c + 1, per_block) == 0, m < blocks))
+        def _():
+            scatter(m)
 
         @pl.when(c >= DELAY)
         def _():

time: 429 us -> 421 us (0.981)
  Pallas kernels: 424 us -> 416 us
    pallas_call x1, Pallas kernels: 402 us -> 395 us  [exchange_and_flow(): pl.pallas_call(functools.partial(fused_kernel, n), out_shape=(out, out),...]
where the time goes in v4:
time: 421 us; the launch traced here: 419 us
  Pallas kernels  416 us (99%)
    pallas_call x1, Pallas kernels, exchange_and_flow(): pl.pallas_call(functools.partial(fused_kernel, n), out_shape=(out, out),...  395 us
    pallas_call x1, Pallas kernels, widen(): pl.pallas_call(widen_kernel, grid=(count // STRIP, rows // STRIP), out_sh...  21.7 us

profile of v4, /device:TPU:13, one launch (start us, length us, event | category | flops | bytes accessed | tf_op | source)
XLA Modules:
  0.0 419.3 jit_solution(14566528026883787157)
XLA Ops:
  0.6 0.8 slice.3
  1.4 0.8 pad_maximum_fusion
  2.1 0.9 broadcast_in_dim.2.power_ref
  3.1 394.5 %exchange.1 = (bf16[64,64,1024]{2,1,0:T(8,128)(2,1)}, bf16[64,64,1024]{2,1,0:T(8,128)(2,1)}) custom-call(bf16[64,64,1024]{2,1,0:T(8,128)(2,1)} %x_ref.1, bf16[512,512]{1,0:T(8,128)(2,1)} %constant.4.clone.basis_ref, bf16[512,512]{1,0:T(8,128)(2,1)} %constant.5.clone.inverse_ref, f32[512,256]{1,0:T(8,128)} %broadcast_in_dim.2.power_ref), custom_call_target="tpu_custom_call" | custom-call | flops 8589934592 | bytes 25165824 | tf_op jit(solution)/shard_map/exchange/pallas_call | solution.py:432
  397.6 21.7 %widen.1 = (f32[64,64,1024]{2,1,0:T(8,128)}, f32[64,64,1024]{2,1,0:T(8,128)}) custom-call(bf16[64,64,1024]{2,1,0:T(8,128)(2,1)} %get-tuple-element.4.u_in, bf16[64,64,1024]{2,1,0:T(8,128)(2,1)} %get-tuple-element.5.v_in), custom_call_target="tpu_custom_call" | custom-call | bytes 50331648 | tf_op jit(solution)/shard_map/widen/pallas_call | solution.py:476
